TPU v7x, 128 devices: a whole 4x4x4 slice. The times are simulated.
128 devices in a mesh: ctx: 16 (over z, y), grp: 8 (over x, core).
Axes of the slice: x: 4, y: 4, z: 4, core: 2. Of those that a mesh axis runs over, the one named last changes fastest.
Arguments:
- tokens: bfloat16 [8192, 7168], P('ctx', 'grp'), may hold values from -6 to 6
- w_dkv: bfloat16 [7168, 576], P('grp'), may hold values from -0.0625 to 0.0625
- latent_gain: float32 [512], replicated, may hold values from 0.25 to 1.75
- q_pre: bfloat16 [8192, 73728], P('ctx', 'grp'), may hold values from -102 to 102
- w_uv: bfloat16 [512, 16384], P(None, 'grp'), may hold values from -0.25 to 0.25
- q_dec: bfloat16 [2, 128, 73728], P(None, 'grp'), may hold values from -102 to 102
- kv_new: bfloat16 [2, 128, 576], P(None, 'grp'), may hold values from -48 to 48
- lengths: int32 [128], P('grp'), may hold values from 1 to 8192
- block_map: int32 [256], replicated, may hold values from 0 to 15, as said below
Outputs:
- prefill_out: bfloat16 [8192, 16384], P('ctx', 'grp')
- decode_cache: bfloat16 [8192, 576], P('ctx')
- decode_out: bfloat16 [2, 128, 65536], P(None, 'grp', 'ctx')
Inputs may be any that keep to these rules, and one draw needn't show every extreme that they name: `block_map`: for each index o of ctx, the 16 entries o*16 to o*16 + 15 name every shard number 0 to 15 exactly once.
All inputs are finite; a program needn't handle non-finite values.
Results may differ from a plain program's by a relative error of at most 0.012.
The roundings to bfloat16 on the way count: a program that leaves them out, or rounds other values in their place, can miss the bound.
Values may be sent and summed in bfloat16 or wider, within the bound.
A program may use at most 128 MiB of HBM per device.

v0:
```python
import jax
import jax.numpy as jnp
from jax import lax
from jax.sharding import PartitionSpec as P

BLOCK = 128


scale_qk = 0.07216878364870322
eps_norm = 1e-06
neg_fill = -1e30


def from_behind(value, axis, steps):
    count = lax.axis_size(axis)
    first, last = (max(0, -steps), min(count, count - steps))
    return lax.ppermute(value, axis, [(source, source + steps) for source in range(first, last)])


def rotate(values, positions):
    half = values.shape[1] // 2
    freqs = 10000.0 ** (-(jnp.arange(half, dtype=jnp.float32) * 2.0) / (2.0 * half))
    angles = positions.astype(jnp.float32)[:, None] * freqs[None, :]
    cosine = jnp.cos(angles)
    sine = jnp.sin(angles)
    first = values[:, :half]
    second = values[:, half:]
    return jnp.concatenate([first * cosine - second * sine, second * cosine + first * sine], axis=1)


def make_rows(summed, gain, positions, rank):
    latent = summed[:, :rank]
    power = jnp.mean(latent * latent, axis=1, keepdims=True)
    normed = latent * lax.rsqrt(power + eps_norm) * gain[None, :]
    return jnp.concatenate([normed, rotate(summed[:, rank:], positions)], axis=1).astype(
        jnp.bfloat16
    )


def shards(tokens, w_dkv, latent_gain, q_pre, w_uv, q_dec, kv_new, lengths, block_map):
    n_ctx = lax.axis_size("ctx")
    me_ctx = lax.axis_index("ctx")
    tok = tokens.shape[0]
    width = w_dkv.shape[1]
    rank = latent_gain.shape[0]
    positions = me_ctx * tok + jnp.arange(tok, dtype=jnp.int32)
    summed = lax.psum(jnp.dot(tokens, w_dkv, preferred_element_type=jnp.float32), "grp")
    rows = make_rows(summed, latent_gain, positions, rank)
    bps = tok // BLOCK
    previous = from_behind(rows[tok - BLOCK :], "ctx", 1)
    extended = jnp.concatenate([previous, rows], axis=0)
    windows = jnp.concatenate(
        [extended[:tok].reshape(bps, BLOCK, width), extended[BLOCK:].reshape(bps, BLOCK, width)],
        axis=1,
    )
    heads_here = q_pre.shape[1] // width
    queries = q_pre.reshape(bps, BLOCK, heads_here, width)
    scores = (
        jnp.einsum("kqhd,kjd->khqj", queries, windows, preferred_element_type=jnp.float32)
        * scale_qk
    )
    block_ids = me_ctx * bps + jnp.arange(bps, dtype=jnp.int32)
    qrow = jnp.arange(BLOCK, dtype=jnp.int32)[:, None]
    kcol = jnp.arange(2 * BLOCK, dtype=jnp.int32)[None, :]
    allowed = jnp.where(
        kcol[None] < BLOCK, block_ids[:, None, None] > 0, (kcol - BLOCK <= qrow)[None]
    )
    allowed = allowed[:, None]
    masked = jnp.where(allowed, scores, neg_fill)
    peak = jnp.max(masked, axis=3, keepdims=True)
    expo = jnp.where(allowed, jnp.exp(masked - peak), 0.0)
    weights = (expo / jnp.sum(expo, axis=3, keepdims=True)).astype(jnp.bfloat16)
    latent_out = jnp.einsum(
        "khqj,kjr->kqhr", weights, windows[:, :, :rank], preferred_element_type=jnp.float32
    ).astype(jnp.bfloat16)
    values_up = w_uv.reshape(rank, heads_here, w_uv.shape[1] // heads_here)
    prefill_out = jnp.einsum(
        "kqhr,rhv->kqhv", latent_out, values_up, preferred_element_type=jnp.float32
    )
    prefill_out = prefill_out.astype(jnp.bfloat16).reshape(tok, w_uv.shape[1])
    page = tok // n_ctx
    pages = rows.reshape(n_ctx, page, width)
    targets = lax.dynamic_slice_in_dim(block_map, me_ctx * n_ctx, n_ctx, 0)
    outgoing = (targets[None, :] == jnp.arange(n_ctx, dtype=jnp.int32)[:, None]).astype(
        jnp.bfloat16
    )
    sending = jnp.einsum("dj,jpl->dpl", outgoing, pages, preferred_element_type=jnp.float32).astype(
        jnp.bfloat16
    )
    arrived = lax.all_to_all(sending, "ctx", split_axis=0, concat_axis=0, tiled=True)
    decode_cache = arrived.reshape(tok, width)
    table = block_map.reshape(n_ctx, n_ctx)
    within = jnp.sum(
        jnp.where(table == me_ctx, jnp.arange(n_ctx, dtype=jnp.int32)[None, :], 0), axis=1
    )
    page_ids = jnp.arange(n_ctx, dtype=jnp.int32) * n_ctx + within
    key_pos = (page_ids[:, None] * page + jnp.arange(page, dtype=jnp.int32)[None, :]).reshape(tok)
    steps = q_dec.shape[0]
    reqs = q_dec.shape[1]
    heads_all = q_dec.shape[2] // width
    dec_q = q_dec.reshape(steps, reqs, heads_all, width)
    dec_scores = (
        jnp.einsum("srhd,jd->srhj", dec_q, decode_cache, preferred_element_type=jnp.float32)
        * scale_qk
    )
    live = (key_pos[None, :] < lengths[:, None])[None, :, None, :]
    dec_masked = jnp.where(live, dec_scores, neg_fill)
    dec_peak = jnp.max(dec_masked, axis=3)
    dec_expo = jnp.where(live, jnp.exp(dec_masked - dec_peak[..., None]), 0.0)
    dec_total = jnp.sum(dec_expo, axis=3)
    dec_acc = jnp.einsum(
        "srhj,jc->srhc",
        dec_expo.astype(jnp.bfloat16),
        decode_cache[:, :rank],
        preferred_element_type=jnp.float32,
    )
    head_count = heads_all // n_ctx
    pieces = (
        lax.all_to_all(dec_peak[None], "ctx", split_axis=3, concat_axis=0, tiled=True),
        lax.all_to_all(dec_total[None], "ctx", split_axis=3, concat_axis=0, tiled=True),
        lax.all_to_all(dec_acc[None], "ctx", split_axis=3, concat_axis=0, tiled=True),
    )
    top = jnp.max(pieces[0], axis=0)
    factors = jnp.exp(pieces[0] - top[None])
    total = jnp.sum(pieces[1] * factors, axis=0)
    acc = jnp.sum(pieces[2] * factors[..., None], axis=0)
    own_q = lax.dynamic_slice_in_dim(dec_q, me_ctx * head_count, head_count, 2)
    new_scores = (
        jnp.einsum("srhd,trd->srht", own_q, kv_new, preferred_element_type=jnp.float32) * scale_qk
    )
    own_mask = (jnp.arange(steps)[None, :] <= jnp.arange(steps)[:, None])[:, None, None, :]
    new_masked = jnp.where(own_mask, new_scores, neg_fill)
    final_top = jnp.maximum(top, jnp.max(new_masked, axis=3))
    old_factor = jnp.exp(top - final_top)
    new_expo = jnp.where(own_mask, jnp.exp(new_masked - final_top[..., None]), 0.0)
    total = total * old_factor + jnp.sum(new_expo, axis=3)
    acc = acc * old_factor[..., None] + jnp.einsum(
        "srht,trc->srhc",
        new_expo.astype(jnp.bfloat16),
        kv_new[:, :, :rank],
        preferred_element_type=jnp.float32,
    )
    decode_out = (
        (acc / total[..., None]).astype(jnp.bfloat16).reshape(steps, reqs, head_count * rank)
    )
    return (prefill_out, decode_cache, decode_out)


def solution(mesh):
    placed = (
        P("ctx", "grp"),
        P("grp", None),
        P(),
        P("ctx", "grp"),
        P(None, "grp"),
        P(None, "grp", None),
        P(None, "grp", None),
        P("grp"),
        P(),
    )
    return jax.shard_map(
        shards,
        mesh=mesh,
        in_specs=placed,
        out_specs=(P("ctx", "grp"), P("ctx", None), P(None, "grp", "ctx")),
        check_vma=False,
    )
```

profile of v0, /device:TPU:30, one launch (start us, length us, event | category | flops | bytes accessed | tf_op | source)
XLA Modules:
  0.0 329.6 jit_solution(7692195456714761228)
XLA Ops:
  7.2 1.2 copy-done
  8.4 3.0 fusion.74
  11.4 0.8 dynamic_slice.6
  12.2 0.7 broadcast_compare_fusion.1
  13.1 61.1 %all-reduce.2.cloned.1.call-done = f32[512,576]{0,1:T(8,128)} async-done(((f32[512,576]{0,1:T(8,128)}), f32[512,576]{0,1:T(8,128)}) %all-reduce.2.cloned.1.call-update) | async-done | bytes 1179664 | tf_op jit(solution)/shard_map/psum | solution.py:47
  74.2 1.2 fusion.55
  75.5 0.2 copy.135
  75.9 0.2 copy.136
  76.1 1.3 multiply_reduce_fusion
  77.4 1.4 multiply_convert_fusion
  78.8 0.2 copy.133
  79.0 0.3 copy.134
  79.3 0.4 convolution_convert_fusion
  79.7 1.0 copy.137
  80.6 7.4 %all-to-all-start = ((bf16[16,32,576]{2,1,0:T(8,128)(2,1)}), bf16[16,32,576]{2,1,0:T(8,128)(2,1)S(1)}, u32[]{:S(2)}, u32[]{:S(2)}) async-start(bf16[16,32,576]{2,1,0:T(8,128)(2,1)} %copy.137), calls=%async_computation | async-start | bytes 1310720 | tf_op jit(solution)/shard_map/all_to_all | solution.py:90
  88.2 8.8 %reshape.199 = bf16[2,16,128,576]{3,2,1,0:T(8,128)(2,1)} reshape(bf16[2,16,73728]{2,1,0:T(8,128)(2,1)} %param.14) | data formatting | bytes 9437184 | tf_op jit(solution)/shard_map/reshape | solution.py:101
  97.1 2.5 all-to-all-done
  99.6 7.7 %fusion.9 = (f32[2,16,128]{2,1,0:T(8,128)S(1)}, f32[512,2,16,128]{3,0,2,1:T(8,128)S(1)}) fusion(pred[16,512]{1,0:T(8,128)(4,1)S(1)} %broadcast_compare_fusion, bf16[512,576,1,1]{1,0,3,2:T(8,128)(2,1)S(1)} %bitcast.143, bf16[2,16,128,576]{3,2,1,0:T(8,128)(2,1)} %reshape.199), kind=kOutput, calls=%fused_computation.14 | convolution fusion | flops 2422206464 | bytes 13721600 | tf_op jit(solution)/shard_map/srhd,jd->srhj/dot_general | solution.py:103
  107.3 3.2 copy-done.4
  110.5 2.5 fusion.11
  113.1 0.8 reshape.212
  113.9 6.5 %all-to-all-start.3 = ((f32[16,1,256]{2,1,0:T(1,128)}), f32[16,1,256]{2,1,0:T(1,128)S(1)}, u32[]{:S(2)}, u32[]{:S(2)}) async-start(f32[16,1,256]{2,1,0:T(1,128)} %reshape.212), calls=%async_computation.3 | async-start | bytes 32768 | tf_op jit(solution)/shard_map/all_to_all | solution.py:120
  120.6 0.8 reshape.210
  121.4 4.7 %all-to-all-done.3 = f32[16,1,256]{2,1,0:T(1,128)S(1)} async-done(((f32[16,1,256]{2,1,0:T(1,128)}), f32[16,1,256]{2,1,0:T(1,128)S(1)}, u32[]{:S(2)}, u32[]{:S(2)}) %all-to-all-start.3) | async-done | bytes 16416 | tf_op jit(solution)/shard_map/all_to_all | solution.py:120
  126.1 5.4 %all-to-all-start.2 = ((f32[16,1,256]{2,1,0:T(1,128)}), f32[16,1,256]{2,1,0:T(1,128)S(1)}, u32[]{:S(2)}, u32[]{:S(2)}) async-start(f32[16,1,256]{2,1,0:T(1,128)} %reshape.210), calls=%async_computation.2 | async-start | bytes 32768 | tf_op jit(solution)/shard_map/all_to_all | solution.py:119
  131.5 7.1 %fusion.25 = f32[1,2,16,128,512]{4,3,2,1,0:T(8,128)S(1)} fusion(f32[512,2,16,128]{3,0,2,1:T(8,128)} %copy-done.4, f32[2,16,128]{2,1,0:T(8,128)S(1)} %get-tuple-element.26, pred[16,512]{1,0:T(8,128)(4,1)S(1)} %broadcast_compare_fusion, bf16[512,576]{1,0:T(8,128)(2,1)S(1)} %bitcast.144), kind=kOutput, calls=%fused_computation.28 | convolution fusion | flops 2157969408 | bytes 17326080 | tf_op jit(solution)/shard_map/srhj,jc->srhc/dot_general | solution.py:111
  138.6 8.1 %copy.141 = f32[1,2,16,128,512]{4,2,1,0,3:T(8,128)} copy(f32[1,2,16,128,512]{4,3,2,1,0:T(8,128)S(1)} %fusion.25) | data formatting | bytes 16777216 | tf_op jit(solution)/shard_map/broadcast_in_dim | solution.py:121
  146.7 7.4 %all-to-all-start.1 = ((f32[1,2,16,128,512]{4,2,1,0,3:T(8,128)}), f32[1,2,16,128,512]{4,2,1,0,3:T(8,128)}, u32[]{:S(2)}, u32[]{:S(2)}) async-start(f32[1,2,16,128,512]{4,2,1,0,3:T(8,128)} %copy.141), calls=%async_computation.1 | async-start | bytes 16777216 | tf_op jit(solution)/shard_map/all_to_all | solution.py:121
  154.1 2.0 fusion.73
  156.2 16.8 %reshape.209 = bf16[4,128,16,576]{3,2,1,0:T(8,128)(2,1)} reshape(bf16[512,9216]{1,0:T(8,128)(2,1)} %param.12) | data formatting | bytes 18874368 | tf_op jit(solution)/shard_map/reshape | solution.py:57
  173.0 3.7 %copy.183 = bf16[64,8,16,128]{3,2,1,0:T(8,128)(2,1)} copy(bf16[64,8,16,128]{3,1,2,0:T(8,128)(2,1)} %bitcast.146) | data formatting | bytes 4194304
  176.8 0.2 broadcast_select_fusion
  177.0 3.7 %collective-permute-start = (bf16[128,576]{0,1:T(8,128)(2,1)S(1)}, bf16[128,576]{0,1:T(8,128)(2,1)S(1)}, u32[]{:S(2)}, u32[]{:S(2)}) collective-permute-start(bf16[128,576]{0,1:T(8,128)(2,1)S(1)} %pad_maximum_fusion.3), channel_id=1, source_target_pairs={{0,8},{8,16},{16,24},{24,32},{32,40},{40,48},{48,56},{56,64},{64,7... | collective-permute-start | bytes 442376 | tf_op jit(solution)/shard_map/ppermute | solution.py:17
  181.0 94.3 %collective-permute-done = bf16[128,576]{0,1:T(8,128)(2,1)S(1)} collective-permute-done((bf16[128,576]{0,1:T(8,128)(2,1)S(1)}, bf16[128,576]{0,1:T(8,128)(2,1)S(1)}, u32[]{:S(2)}, u32[]{:S(2)}) %collective-permute-start) | collective-permute-done | bytes 147488 | tf_op jit(solution)/shard_map/ppermute | solution.py:17
  275.5 6.6 %fusion.1 = f32[4,256,128,16]{2,1,3,0:T(8,128)} fusion(bf16[4,128,16,576]{3,2,1,0:T(8,128)(2,1)S(1)} %copy-done.2, bf16[4,128,32]{1,2,0:T(8,128)(2,1)S(1)} %get-tuple-element.30, bf16[4,128,32]{1,2,0:T(8,128)(2,1)S(1)} %get-tuple-element.31, bf16[4,128,512]{1,2,0:T(8,128)(2,1)S(1)} %copy_bitcast_fusion.2, bf16[4,128,576]{1,2,0:T(8,128)(2,1)S(1)} %copy_bitcast_fusion.1), kind=kOutput, calls=%fused_computation.1 | convolution fusion | flops 2420637696 | bytes 19005440 | tf_op jit(solution)/shard_map/kqhd,kjd->khqj/dot_general | solution.py:59
  282.1 12.3 %fusion.72 = (f32[4,16,128]{2,1,0:T(8,128)S(1)}, f32[4,16,128,256]{2,3,1,0:T(8,128)}) fusion(f32[4,256,128,16]{2,1,3,0:T(8,128)} %fusion.1, pred[4,128,256]{1,2,0:T(8,128)(4,1)S(1)} %broadcast_select_fusion), kind=kOutput, calls=%fused_computation.110 | output fusion | flops 14680319 | bytes 16941056 | tf_op jit(solution)/shard_map/sub | solution.py:71
  294.4 8.9 %convert_bitcast_fusion = bf16[4,128,16,128]{3,1,0,2:T(8,128)(2,1)} fusion(bf16[512,16,128,1]{2,1,0,3:T(8,128)(2,1)} %bitcast.148, bf16[4,256,576]{1,2,0:T(8,128)(2,1)S(1)} %maximum_maximum_fusion, f32[4,16,128,256]{2,3,1,0:T(8,128)} %get-tuple-element.25, f32[4,16,128]{2,1,0:T(8,128)S(1)} %get-tuple-element.24), kind=kOutput, calls=%fused_computation.31 | convolution fusion | flops 3230662656 | bytes 13664256 | tf_op jit(solution)/shard_map/kqhr,rhv->kqhv/dot_general | solution.py:77
  303.3 2.9 copy.132
  306.2 1.9 copy.219
  308.1 1.1 copy.157
  309.1 0.5 broadcast.149
  309.6 0.7 reduce.1
  310.3 0.2 reshape.213
  310.5 0.7 reduce.2
  311.2 0.2 reshape.211
  312.2 9.1 %fusion.3 = f32[2,16,8,512]{3,2,1,0:T(8,128)S(1)} fusion(f32[1,2,16,16,8,512]{5,2,1,4,3,0:T(8,128)} %bitcast.15, f32[16,2,16,8]{3,0,2,1:T(8,128)S(1)} %copy.145), kind=kLoop, calls=%fused_computation.4 | loop fusion | flops 4063232 | bytes 8929280 | tf_op jit(solution)/shard_map/reduce_sum | solution.py:126
  321.3 0.4 fusion.37
  321.9 0.9 copy.158
  (54 shorter events, 2.5 us)
Async XLA Ops:
  7.2 1.2 copy-start
  7.2 70.2 %copy-start.6 = (f32[512]{0:T(512)S(1)}, f32[512]{0:T(512)}, u32[]{:S(2)}) copy-start(f32[512]{0:T(512)} %param.11) | copy-start | bytes 6148
  7.2 67.0 %all-reduce.2.cloned.1.call-start = ((), (), s32[]{:S(2)}) async-start(), calls=%async_computation.4 | async-start | bytes 2359296 | tf_op jit(solution)/shard_map/psum | solution.py:47
  80.6 18.9 %all-to-all-start = ((bf16[16,32,576]{2,1,0:T(8,128)(2,1)}), bf16[16,32,576]{2,1,0:T(8,128)(2,1)S(1)}, u32[]{:S(2)}, u32[]{:S(2)}) async-start(bf16[16,32,576]{2,1,0:T(8,128)(2,1)} %copy.137), calls=%async_computation | async-start | bytes 1310720 | tf_op jit(solution)/shard_map/all_to_all | solution.py:90
  88.0 9.0 %copy-start.7 = (s32[16]{0:T(128)S(1)}, s32[16]{0:T(128)}, u32[]{:S(2)}) copy-start(s32[16]{0:T(128)} %param.16) | copy-start | bytes 196
  107.3 3.2 copy-start.4
  113.9 12.2 %all-to-all-start.3 = ((f32[16,1,256]{2,1,0:T(1,128)}), f32[16,1,256]{2,1,0:T(1,128)S(1)}, u32[]{:S(2)}, u32[]{:S(2)}) async-start(f32[16,1,256]{2,1,0:T(1,128)} %reshape.212), calls=%async_computation.3 | async-start | bytes 32768 | tf_op jit(solution)/shard_map/all_to_all | solution.py:120
  126.1 20.6 %all-to-all-start.2 = ((f32[16,1,256]{2,1,0:T(1,128)}), f32[16,1,256]{2,1,0:T(1,128)S(1)}, u32[]{:S(2)}, u32[]{:S(2)}) async-start(f32[16,1,256]{2,1,0:T(1,128)} %reshape.210), calls=%async_computation.2 | async-start | bytes 32768 | tf_op jit(solution)/shard_map/all_to_all | solution.py:119
  146.7 7.4 %copy-start.5 = (bf16[2,16,576]{2,1,0:T(8,128)(2,1)S(1)}, bf16[2,16,576]{2,1,0:T(8,128)(2,1)}, u32[]{:S(2)}) copy-start(bf16[2,16,576]{2,1,0:T(8,128)(2,1)} %param.15) | copy-start | bytes 110596
  146.7 165.5 %all-to-all-start.1 = ((f32[1,2,16,128,512]{4,2,1,0,3:T(8,128)}), f32[1,2,16,128,512]{4,2,1,0,3:T(8,128)}, u32[]{:S(2)}, u32[]{:S(2)}) async-start(f32[1,2,16,128,512]{4,2,1,0,3:T(8,128)} %copy.141), calls=%async_computation.1 | async-start | bytes 16777216 | tf_op jit(solution)/shard_map/all_to_all | solution.py:121
  156.2 24.6 %copy-start.3 = (f32[512,576]{0,1:T(8,128)S(1)}, f32[512,576]{0,1:T(8,128)}, u32[]{:S(2)}) copy-start(f32[512,576]{0,1:T(8,128)} %all-reduce.2.cloned.1.call-done) | copy-start | bytes 3538948
  173.0 102.5 %copy-start.2 = (bf16[4,128,16,576]{3,2,1,0:T(8,128)(2,1)S(1)}, bf16[4,128,16,576]{3,2,1,0:T(8,128)(2,1)}, u32[]{:S(2)}) copy-start(bf16[4,128,16,576]{3,2,1,0:T(8,128)(2,1)} %reshape.209) | copy-start | bytes 28311556
  177.0 98.2 %collective-permute-start = (bf16[128,576]{0,1:T(8,128)(2,1)S(1)}, bf16[128,576]{0,1:T(8,128)(2,1)S(1)}, u32[]{:S(2)}, u32[]{:S(2)}) collective-permute-start(bf16[128,576]{0,1:T(8,128)(2,1)S(1)} %pad_maximum_fusion.3), channel_id=1, source_target_pairs={{0,8},{8,16},{16,24},{24,32},{32,40},{40,48},{48,56},{56,64},{64,7... | collective-permute-start | bytes 442376 | tf_op jit(solution)/shard_map/ppermute | solution.py:17
  312.2 10.6 %copy-start.1 = (bf16[896,576]{0,1:T(8,128)(2,1)S(1)}, bf16[896,576]{0,1:T(8,128)(2,1)}, u32[]{:S(2)}) copy-start(bf16[896,576]{0,1:T(8,128)(2,1)} %param.10) | copy-start | bytes 3096580
Sparse Core Ops, SparseCore 0:
  11.5 62.5 all-reduce.1
where the time goes:
time: 331 us; the launch traced here: 330 us
  waiting for transfers between devices  163 us (49%)
  local copies, waits for them, and re-layouts  55 us (17%)
  matrix products  36 us (11%)
  other arithmetic  31.1 us (9%)
  starting transfers between devices  30.4 us (9%)
  between operations  14.4 us (4%)
    ppermute x1, waiting for transfers between devices, from_behind(): lax.ppermute(value, axis, [(source, source + steps) for source in range(f...  94.3 us
    psum x1, waiting for transfers between devices, shards(): lax.psum(jnp.dot(tokens, w_dkv, preferred_element_type=jnp.float32), 'grp')  61.1 us
    reshape x1, local copies, waits for them, and re-layouts, shards(): queries = q_pre.reshape(bps, BLOCK, heads_here, width)  16.8 us
    unnamed x24, local copies, waits for them, and re-layouts  13.9 us
    sub x1, other arithmetic, shards(): expo = jnp.where(allowed, jnp.exp(masked - peak), 0.0)  12.3 us
    reduce_sum x1, other arithmetic, shards(): acc = jnp.sum(pieces[2] * factors[..., None], axis=0)  9.15 us
    dot_general x1, matrix products, shards(): jnp.einsum('kqhr,rhv->kqhv', latent_out, values_up, preferred_element_typ...  8.9 us
    reshape x1, local copies, waits for them, and re-layouts, shards(): dec_q = q_dec.reshape(steps, reqs, heads_all, width)  8.81 us
  transfers between devices with their start and end apart: 6, of which 4 were waited for; matrix products, arithmetic and copies ran while one was open for 26% of the time, Pallas kernels for 0%

commit v1 on v0

v1 whole, which is shorter than its diff:
```python
import math

import jax
import jax.numpy as jnp
import numpy as np
from jax import lax
from jax.experimental import pallas as pl
from jax.experimental.pallas import tpu as pltpu
from jax.sharding import PartitionSpec as P

MESH = pl.DeviceIdType.MESH
F32 = jnp.float32
BF16 = jnp.bfloat16

scale_qk = 0.07216878364870322
eps_norm = 1e-06
neg_fill = -1e30
EXP2_SCALE = scale_qk * math.log2(math.e)

RANK = 512
WIDTH = 576
WIDE = 640
ROPE = 64
BLOCK = 128
PIECE = 16
GROUPS = 4
GROUP_ROWS = 1024
HEADS = 16
DEC_HEADS = 8

ORDERS = (
    ("yzx", "zyx"),
    ("zxy", "xzy"),
    ("yxz", "xyz"),
    ("xzy", "xyz"),
)
POS_STRIDE = {"z": 2048, "y": 512, "x": 32}
SLOT_STRIDE = (PIECE, 4 * PIECE, 16 * PIECE)
DELTAS = (1, 3, 2)
FREQS = [float(np.float32(10000.0 ** (-2.0 * i / ROPE))) for i in range(ROPE // 2)]


def dot_nt(a, b):
    return lax.dot_general(a, b, (((1,), (1,)), ((), ())), preferred_element_type=F32)


def dot_nn(a, b):
    return jnp.dot(a, b, preferred_element_type=F32)


def kernel(
    tokens,
    w_dkv,
    gain,
    q_pre,
    w_uv,
    q_dec,
    kv_new,
    lengths,
    block_map,
    o_pre,
    o_cache,
    o_dec,
    tok_v,
    w_v,
    q_v,
    uv_v,
    qd_v,
    kv_v,
    part,
    from_core,
    chip_sum,
    from_x,
    buf,
    win,
    qs,
    kn,
    acc,
    top,
    total,
    out_v,
    cache_v,
    dec_v,
    load_sem,
    core_send,
    core_recv,
    x_send,
    x_recv,
    g_send,
    g_recv,
    f_send,
    f_recv,
    out_sem,
):
    ctx = lax.axis_index("ctx")
    grp = lax.axis_index("grp")
    at = {"z": ctx // 4, "y": lax.rem(ctx, 4), "x": grp // 2}
    core = lax.rem(grp, 2)
    other = 1 - core

    def device(x, y, z, c):
        return (z * 4 + y, x * 2 + c)

    def moved(axis, delta):
        new = dict(at)
        new[axis] = lax.rem(at[axis] + delta, 4)
        return device(new["x"], new["y"], new["z"], core)

    sibling = device(at["x"], at["y"], at["z"], other)

    loads = {
        "tok": pltpu.make_async_copy(tokens, tok_v, load_sem.at[0]),
        "w": pltpu.make_async_copy(w_dkv, w_v, load_sem.at[1]),
        "qd": pltpu.make_async_copy(
            q_dec.at[:, :, pl.ds(pl.multiple_of(ctx * (DEC_HEADS * WIDTH), 128), DEC_HEADS * WIDTH)],
            qd_v,
            load_sem.at[2],
        ),
        "kv": pltpu.make_async_copy(kv_new, kv_v, load_sem.at[3]),
        "q": pltpu.make_async_copy(q_pre, q_v, load_sem.at[4]),
        "uv": pltpu.make_async_copy(w_uv, uv_v, load_sem.at[5]),
    }
    for load in loads.values():
        load.start()

    barrier = pltpu.get_barrier_semaphore()
    peers = [sibling] + [moved(axis, delta) for axis in "xyz" for delta in DELTAS]
    for peer in peers:
        pl.semaphore_signal(barrier, inc=1, device_id=peer, device_id_type=MESH)

    def remote(src, dst, send, recv, to):
        return pltpu.make_async_remote_copy(
            src_ref=src, dst_ref=dst, send_sem=send, recv_sem=recv, device_id=to, device_id_type=MESH
        )

    lane = lax.broadcasted_iota(jnp.int32, (PIECE, 128), 1)
    row = lax.broadcasted_iota(jnp.int32, (PIECE, 128), 0)
    freq = jnp.zeros((PIECE, 128), F32)
    for i, value in enumerate(FREQS):
        freq = jnp.where(lane % 32 == i, value, freq)
    tables = []
    for g in range(GROUPS):
        position = ctx * 512 + g * BLOCK + grp * PIECE + row
        angle = position.astype(F32) * freq
        cosine = jnp.where(lane < ROPE, jnp.cos(angle), 0.0)
        sine = jnp.where(lane < ROPE, jnp.sin(angle), 0.0)
        tables.append((cosine, jnp.where(lane < 32, -sine, sine)))

    loads["tok"].wait()
    loads["w"].wait()

    core_copies = []
    for g in range(GROUPS):
        product = dot_nt(tok_v[g * BLOCK : (g + 1) * BLOCK, :], w_v[...])
        for x in range(4):
            for c in range(2):
                at_row = (x * 2 + c) * PIECE
                part[g, c, x * PIECE : (x + 1) * PIECE, :] = product[at_row : at_row + PIECE]
        if g == 0:
            pl.semaphore_wait(barrier, len(peers))
        copy = remote(part.at[g, other], from_core.at[g], core_send.at[g], core_recv.at[g], sibling)
        copy.start()
        core_copies.append(copy)

    x_copies = []
    for g in range(GROUPS):
        core_copies[g].wait_recv()
        chip_sum[g] = part[g, core] + from_core[g]
        for i, delta in enumerate(DELTAS):
            to_x = lax.rem(at["x"] + delta, 4)
            copy = remote(
                chip_sum.at[g, pl.ds(pl.multiple_of(to_x * PIECE, PIECE), PIECE)],
                from_x.at[g, i],
                x_send.at[g * 3 + i],
                x_recv.at[g * 3 + i],
                moved("x", delta),
            )
            copy.start()
            x_copies.append(copy)

    sends = []

    def place(g, k):
        first, second = ORDERS[g][0][k], ORDERS[g][1][k]
        if first == second:
            return at[first]
        return jnp.where(core == 0, at[first], at[second])

    def toward(g, k, delta):
        first, second = ORDERS[g][0][k], ORDERS[g][1][k]
        new = dict(at)
        if first == second:
            new[first] = lax.rem(at[first] + delta, 4)
        else:
            new[first] = lax.rem(at[first] + delta * (1 - core), 4)
            new[second] = lax.rem(at[second] + delta * core, 4)
        return device(new["x"], new["y"], new["z"], core)

    def base(g, plane):
        return (plane * GROUPS + g) * GROUP_ROWS

    def rows_at(start, count):
        return buf.at[pl.ds(pl.multiple_of(start, PIECE), count)]

    def gather_send(g, slot, start, count, k, delta):
        copy = remote(
            rows_at(start, count),
            rows_at(start, count),
            g_send.at[g * 12 + slot],
            g_recv.at[g * 12 + slot],
            toward(g, k, delta),
        )
        copy.start()
        sends.append(copy)

    def gather_wait(g, slot, start, count):
        remote(
            rows_at(start, count),
            rows_at(start, count),
            g_send.at[g * 12 + slot],
            g_recv.at[g * 12 + slot],
            sibling,
        ).wait_recv()

    def pass_on(g, slot, start, count):
        copy = remote(
            rows_at(start, count), rows_at(start, count), f_send.at[g * 7 + slot], f_recv.at[g * 7 + slot], sibling
        )
        copy.start()
        sends.append(copy)

    spots = []
    for g in range(GROUPS):
        spots.append(tuple(place(g, k) for k in range(3)))

    def finish_sum(g):
        for i in range(3):
            x_copies[g * 3 + i].wait_recv()
        summed = (
            chip_sum[g, pl.ds(pl.multiple_of(at["x"] * PIECE, PIECE), PIECE), :]
            + from_x[g, 0]
            + from_x[g, 1]
            + from_x[g, 2]
        )
        latent = summed[:, :RANK]
        power = jnp.mean(latent * latent, axis=1, keepdims=True)
        normed = latent * lax.rsqrt(power + eps_norm) * gain[...]
        tail = summed[:, RANK:]
        pair = jnp.concatenate([tail, tail], axis=1)
        swapped = jnp.where(lane < 32, pltpu.roll(pair, 96, 1), pltpu.roll(pair, 32, 1))
        cosine, sine = tables[g]
        turned = pair * cosine + swapped * sine
        own = base(g, core) + spots[g][2] * 256 + spots[g][1] * 64 + spots[g][0] * 16
        here = pl.ds(pl.multiple_of(own, PIECE), PIECE)
        buf[here, :RANK] = normed.astype(BF16)
        buf[here, RANK:] = turned.astype(BF16)

    def phase1(g):
        own = base(g, core) + spots[g][2] * 256 + spots[g][1] * 64 + spots[g][0] * 16
        for i, delta in enumerate(DELTAS):
            gather_send(g, i, own, PIECE, 0, delta)

    def phase2(g):
        line = base(g, core) + spots[g][2] * 256 + spots[g][1] * 64
        for i, delta in enumerate(DELTAS):
            gather_wait(g, i, line + lax.rem(spots[g][0] + 4 - delta, 4) * 16, PIECE)
        for i, delta in enumerate(DELTAS):
            gather_send(g, 3 + i, line, 64, 1, delta)

    def half(g, offset, h):
        return base(g, core) + lax.rem(spots[g][2] + offset, 4) * 256 + h * 128

    def phase3(g):
        plane = base(g, core) + spots[g][2] * 256
        for i, delta in enumerate(DELTAS):
            gather_wait(g, 3 + i, plane + lax.rem(spots[g][1] + 4 - delta, 4) * 64, 64)
        gather_send(g, 6, half(g, 0, 0), 128, 2, 1)
        gather_send(g, 7, half(g, 0, 1), 128, 2, 3)
        gather_send(g, 8, half(g, 0, 1), 128, 2, 1)
        gather_send(g, 9, half(g, 0, 0), 128, 2, 3)
        pass_on(g, 0, plane, 256)

    def forward(g):
        gather_wait(g, 6, half(g, 3, 0), 128)
        gather_send(g, 10, half(g, 3, 0), 128, 2, 1)
        gather_wait(g, 7, half(g, 1, 1), 128)
        gather_send(g, 11, half(g, 1, 1), 128, 2, 3)
        pass_on(g, 1, half(g, 3, 0), 128)
        pass_on(g, 2, half(g, 1, 1), 128)

    def near(g):
        gather_wait(g, 8, half(g, 3, 1), 128)
        pass_on(g, 3, half(g, 3, 1), 128)
        gather_wait(g, 9, half(g, 1, 0), 128)
        pass_on(g, 4, half(g, 1, 0), 128)

    def far(g):
        gather_wait(g, 10, half(g, 2, 0), 128)
        pass_on(g, 5, half(g, 2, 0), 128)
        gather_wait(g, 11, half(g, 2, 1), 128)
        pass_on(g, 6, half(g, 2, 1), 128)

    def passed(g, slots):
        for slot in slots:
            count = 256 if slot == 0 else 128
            start = base(g, other)
            remote(
                rows_at(start, count), rows_at(start, count), f_send.at[g * 7 + slot], f_recv.at[g * 7 + slot], sibling
            ).wait_recv()

    def copy_window(g, slot, where):
        for x in range(4):
            for c in range(2):
                start = base(g, c)
                for axis, stride in zip(ORDERS[g][c], SLOT_STRIDE, strict=True):
                    start = start + (x if axis == "x" else where[axis]) * stride
                piece = buf[pl.ds(pl.multiple_of(start, PIECE), PIECE), :]
                target = slot * BLOCK + (x * 2 + c) * PIECE
                win[0, target : target + PIECE, :] = piece
                win[1, target : target + PIECE, :] = pltpu.roll(piece.astype(F32), 64, 1).astype(BF16)

    def prefill(b):
        first = ctx * 4 + b
        qrow = lax.rem(lax.broadcasted_iota(jnp.int32, (4 * BLOCK, 2 * BLOCK), 0), BLOCK)
        kcol = lax.broadcasted_iota(jnp.int32, (4 * BLOCK, 2 * BLOCK), 1)
        floor = jnp.where(first > 0, 0, BLOCK)
        allowed = (kcol >= floor) & (kcol - BLOCK <= qrow)
        values = win[0, b * BLOCK : (b + 2) * BLOCK, :RANK]

        def quad(j, carry):
            for odd in range(2):
                queries = jnp.concatenate(
                    [
                        q_v[
                            b * BLOCK : (b + 1) * BLOCK,
                            pl.ds(pl.multiple_of(j * (8 * WIDTH) + p * (2 * WIDTH) + odd * RANK, 128), WIDE),
                        ]
                        for p in range(4)
                    ],
                    axis=0,
                )
                scores = dot_nt(queries, win[odd, b * BLOCK : (b + 2) * BLOCK, :])
                scores = jnp.where(allowed, scores, neg_fill)
                peak = jnp.max(scores, axis=1, keepdims=True)
                expo = jnp.exp2((scores - peak) * EXP2_SCALE)
                share = 1.0 / jnp.sum(expo, axis=1, keepdims=True)
                weights = (expo * share).astype(BF16)
                latent = dot_nn(weights, values).astype(BF16)
                for p in range(4):
                    column = pl.ds(pl.multiple_of(j * 1024 + (2 * p + odd) * 128, 128), 128)
                    result = dot_nn(latent[p * BLOCK : (p + 1) * BLOCK], uv_v[:, column])
                    out_v[b * BLOCK : (b + 1) * BLOCK, column] = result.astype(BF16)
            return carry

        lax.fori_loop(0, 2, quad, 0)
        out = pltpu.make_async_copy(
            out_v.at[pl.ds(b * BLOCK, BLOCK)], o_pre.at[pl.ds(b * BLOCK, BLOCK)], out_sem.at[b]
        )
        out.start()
        return out

    def decode_start():
        loads["qd"].wait()
        loads["kv"].wait()
        wide = lax.broadcasted_iota(jnp.int32, (PIECE, WIDE), 1)
        for h in range(DEC_HEADS):
            for s in range(2):
                column = (h // 2) * (2 * WIDTH) + (h % 2) * RANK
                piece = qd_v[s, :, column : column + WIDE].astype(F32)
                if h % 2:
                    piece = pltpu.roll(piece, WIDE - 64, 1)
                piece = jnp.where(wide < WIDTH, piece, 0.0)
                qs[h * 32 + s * 16 : h * 32 + (s + 1) * 16, :] = piece.astype(BF16)
        kn[...] = jnp.zeros_like(kn)
        for t in range(2):
            kn[t * 16 : (t + 1) * 16, :WIDTH] = kv_v[t]
        rows = lax.broadcasted_iota(jnp.int32, (256, 32), 0)
        cols = lax.broadcasted_iota(jnp.int32, (256, 32), 1)
        allowed = (lax.rem(rows, 16) == lax.rem(cols, 16)) & (cols // 16 <= lax.rem(rows, 32) // 16)
        scores = jnp.where(allowed, dot_nt(qs[...], kn[...]), neg_fill)
        peak = jnp.max(scores, axis=1, keepdims=True)
        expo = jnp.exp2((scores - peak) * EXP2_SCALE)
        top[...] = jnp.broadcast_to(peak, (256, 128))
        total[...] = jnp.broadcast_to(jnp.sum(expo, axis=1, keepdims=True), (256, 128))
        acc[...] = dot_nn(expo.astype(BF16), kn[:, :RANK])

    request = lax.rem(lax.broadcasted_iota(jnp.int32, (256, 1), 0), 16)
    limit = jnp.zeros((256, 1), jnp.int32)
    for r in range(16):
        limit = jnp.where(request == r, lengths[r], limit)

    def decode_chunk(plane, g):
        start = base(g, plane)
        key = lax.broadcasted_iota(jnp.int32, (1, GROUP_ROWS), 1)
        position = g * BLOCK + plane * PIECE + lax.rem(key, PIECE)
        for axis, stride in zip(ORDERS[g][plane], SLOT_STRIDE, strict=True):
            position = position + lax.rem(key // stride, 4) * POS_STRIDE[axis]
        scores = dot_nt(qs[...], buf[start : start + GROUP_ROWS, :])
        scores = jnp.where(position < limit, scores, neg_fill)
        before = top[:, :1]
        peak = jnp.maximum(before, jnp.max(scores, axis=1, keepdims=True))
        factor = jnp.exp2((before - peak) * EXP2_SCALE)
        expo = jnp.exp2((scores - peak) * EXP2_SCALE)
        top[...] = jnp.broadcast_to(peak, (256, 128))
        total[...] = total[...] * factor + jnp.sum(expo, axis=1, keepdims=True)
        acc[...] = acc[...] * factor + dot_nn(expo.astype(BF16), buf[start : start + GROUP_ROWS, :RANK])

    def pick_pages(plane, g):
        for owner in range(16):
            target = owner * 32 + plane * PIECE
            piece = cache_v[target : target + PIECE, :] if g else jnp.zeros((PIECE, WIDTH), BF16)
            where = {"y": owner % 4, "z": owner // 4}
            for x in range(4):
                start = base(g, plane)
                for axis, stride in zip(ORDERS[g][plane], SLOT_STRIDE, strict=True):
                    start = start + (x if axis == "x" else where[axis]) * stride
                mine = block_map[owner * 16 + g * 4 + x] == ctx
                piece = jnp.where(mine, buf[start : start + PIECE, :WIDTH], piece)
            cache_v[target : target + PIECE, :] = piece

    def decode_end():
        result = (acc[...] / total[:, :1]).astype(BF16)
        for h in range(DEC_HEADS):
            for s in range(2):
                at_row = h * 32 + s * 16
                dec_v[s, :, h * RANK : (h + 1) * RANK] = result[at_row : at_row + 16]

    finish_sum(0)
    phase1(0)
    finish_sum(1)
    phase1(1)
    finish_sum(2)
    phase1(2)
    phase2(0)
    finish_sum(3)
    phase1(3)
    phase2(1)
    phase2(2)
    phase3(0)
    phase2(3)
    phase3(1)
    phase3(2)
    phase3(3)
    decode_start()
    loads["q"].wait()
    loads["uv"].wait()
    for g in range(GROUPS):
        passed(g, (0,))
    copy_window(1, 2, at)
    copy_window(2, 3, at)
    copy_window(3, 4, at)
    outs = []
    outs.append(prefill(2))
    for g in range(GROUPS):
        forward(g)
    outs.append(prefill(3))
    for g in range(GROUPS):
        near(g)
    for g in range(GROUPS):
        far(g)
    for g in range(GROUPS):
        passed(g, range(1, 7))
    copy_window(0, 1, at)
    behind = lax.rem(ctx + 15, 16)
    copy_window(3, 0, {"z": behind // 4, "y": lax.rem(behind, 4)})
    outs.append(prefill(1))
    outs.append(prefill(0))
    for plane in range(2):
        for g in range(GROUPS):
            decode_chunk(plane, g)
            pick_pages(plane, g)
    out = pltpu.make_async_copy(cache_v, o_cache, out_sem.at[4])
    out.start()
    outs.append(out)
    decode_end()
    out = pltpu.make_async_copy(dec_v, o_dec, out_sem.at[5])
    out.start()
    outs.append(out)
    for copy in core_copies + x_copies + sends:
        copy.wait_send()
    for out in outs:
        out.wait()


def shards(tokens, w_dkv, latent_gain, q_pre, w_uv, q_dec, kv_new, lengths, block_map):
    anywhere = pl.BlockSpec(memory_space=pl.ANY)
    vmem = pl.BlockSpec(memory_space=pltpu.VMEM)
    smem = pl.BlockSpec(memory_space=pltpu.SMEM)
    sems = pltpu.SemaphoreType.DMA
    return pl.pallas_call(
        kernel,
        out_shape=(
            jax.ShapeDtypeStruct((512, 2048), BF16),
            jax.ShapeDtypeStruct((512, WIDTH), BF16),
            jax.ShapeDtypeStruct((2, 16, 4096), BF16),
        ),
        in_specs=[anywhere, anywhere, vmem, anywhere, anywhere, anywhere, anywhere, smem, smem],
        out_specs=(anywhere, anywhere, anywhere),
        scratch_shapes=[
            pltpu.VMEM((512, 896), BF16),
            pltpu.VMEM((WIDTH, 896), BF16),
            pltpu.VMEM((512, HEADS * WIDTH), BF16),
            pltpu.VMEM((RANK, 2048), BF16),
            pltpu.VMEM((2, 16, DEC_HEADS * WIDTH), BF16),
            pltpu.VMEM((2, 16, WIDTH), BF16),
            pltpu.VMEM((GROUPS, 2, 64, WIDTH), F32),
            pltpu.VMEM((GROUPS, 64, WIDTH), F32),
            pltpu.VMEM((GROUPS, 64, WIDTH), F32),
            pltpu.VMEM((GROUPS, 3, PIECE, WIDTH), F32),
            pltpu.VMEM((2 * GROUPS * GROUP_ROWS, WIDE), BF16),
            pltpu.VMEM((2, 5 * BLOCK, WIDE), BF16),
            pltpu.VMEM((256, WIDE), BF16),
            pltpu.VMEM((32, WIDE), BF16),
            pltpu.VMEM((256, RANK), F32),
            pltpu.VMEM((256, 128), F32),
            pltpu.VMEM((256, 128), F32),
            pltpu.VMEM((512, 2048), BF16),
            pltpu.VMEM((512, WIDTH), BF16),
            pltpu.VMEM((2, 16, 4096), BF16),
            sems((6,)),
            sems((GROUPS,)),
            sems((GROUPS,)),
            sems((GROUPS * 3,)),
            sems((GROUPS * 3,)),
            sems((GROUPS * 12,)),
            sems((GROUPS * 12,)),
            sems((GROUPS * 7,)),
            sems((GROUPS * 7,)),
            sems((6,)),
        ],
        compiler_params=pltpu.CompilerParams(
            collective_id=0, has_side_effects=True, vmem_limit_bytes=56 * 1024 * 1024
        ),
    )(tokens, w_dkv.T, latent_gain.reshape(1, RANK), q_pre, w_uv, q_dec, kv_new, lengths, block_map)


def solution(mesh):
    placed = (
        P("ctx", "grp"),
        P("grp", None),
        P(),
        P("ctx", "grp"),
        P(None, "grp"),
        P(None, "grp", None),
        P(None, "grp", None),
        P("grp"),
        P(),
    )
    return jax.shard_map(
        shards,
        mesh=mesh,
        in_specs=placed,
        out_specs=(P("ctx", "grp"), P("ctx", None), P(None, "grp", "ctx")),
        check_vma=False,
    )
```

time: 331 us -> 77.2 us (0.23)
  the two profiles are of different devices: /device:TPU:30 before, /device:TPU:1 now
where the time goes in v1:
time: 77.2 us; the launch traced here: 77 us
  Pallas kernels  70.3 us (91%)
  local copies, waits for them, and re-layouts  6.04 us (8%)
    pallas_call x1, Pallas kernels, shards(): pl.pallas_call(kernel, out_shape=(jax.ShapeDtypeStruct((512, 2048), BF16)...  70.3 us
    unnamed x4, local copies, waits for them, and re-layouts  3.91 us
    pallas_call x1, local copies, waits for them, and re-layouts, shards(): pl.pallas_call(kernel, out_shape=(jax.ShapeDtypeStruct((512, 2048), BF16)...  2.13 us

profile of v1, /device:TPU:1, one launch (start us, length us, event | category | flops | bytes accessed | tf_op | source)
XLA Modules:
  0.0 77.0 jit_solution(10490122863811482779)
XLA Ops:
  0.6 70.3 %shard_map.112 = (bf16[512,2048]{1,0:T(8,128)(2,1)}, bf16[512,576]{1,0:T(8,128)(2,1)}, bf16[2,16,4096]{2,1,0:T(8,128)(2,1)}) custom-call(bf16[512,896]{1,0:T(8,128)(2,1)} %tokens.1, bf16[576,896]{1,0:T(8,128)(2,1)} %bitcast.2, f32[1,512]{1,0:T(1,128)} %bitcast.3, bf16[512,9216]{1,0:T(8,128)(2,1)} %q_pre.1, bf16[512,2048]{1,0:T(8,128)(2,1)} %w_uv.1, ...), custom_call_target="tpu_custom_call" | custom-call | tf_op jit(solution)/shard_map/pallas_call | solution.py:490
  71.0 2.1 %copy.12 = bf16[512,576]{0,1:T(8,128)(2,1)} copy(bf16[512,576]{1,0:T(8,128)(2,1)} %get-tuple-element.4) | data formatting | bytes 1179648 | tf_op jit(solution)/shard_map/pallas_call | solution.py:490
  73.1 0.0 copy-start
  73.1 3.2 %copy.15 = bf16[512,2048]{1,0:T(8,128)(2,1)} copy(bf16[512,2048]{1,0:T(8,128)(2,1)} %get-tuple-element.9) | data formatting | bytes 4194304
  76.3 0.0 copy-done
  76.3 0.7 copy.16
Async XLA Ops:
  73.1 3.2 %copy-start = (bf16[2,16,4096]{2,1,0:T(8,128)(2,1)S(1)}, bf16[2,16,4096]{2,1,0:T(8,128)(2,1)}, u32[]{:S(2)}) copy-start(bf16[2,16,4096]{2,1,0:T(8,128)(2,1)} %get-tuple-element.11) | copy-start | bytes 786436

commit v2 on v1

--- a/solution.py
+++ b/solution.py
@@ -34,6 +34,7 @@
     ("yxz", "xyz"),
     ("xzy", "xyz"),
 )
+ROW_BLOCK = (3, 0, 1, 2)
 POS_STRIDE = {"z": 2048, "y": 512, "x": 32}
 SLOT_STRIDE = (PIECE, 4 * PIECE, 16 * PIECE)
 DELTAS = (1, 3, 2)
@@ -46,6 +47,39 @@
 
 def dot_nn(a, b):
     return jnp.dot(a, b, preferred_element_type=F32)
+
+
+def base(g, plane):
+    return (plane * GROUPS + g) * GROUP_ROWS
+
+
+def attend(parts, at, lengths, buf, qs, acc, top, total):
+    request = lax.rem(lax.broadcasted_iota(jnp.int32, (256, 1), 0), 16)
+    limit = jnp.zeros((256, 1), jnp.int32)
+    for r in range(16):
+        limit = jnp.where(request == r, lengths[r], limit)
+    spans, masks = [], []
+    for plane, g, offset in parts:
+        order = ORDERS[g][plane]
+        count = GROUP_ROWS if offset is None else 256
+        last = 0 if offset is None else lax.rem(at[order[2]] + offset, 4)
+        spans.append(pl.ds(pl.multiple_of(base(g, plane) + last * 256, 256), count))
+        key = lax.broadcasted_iota(jnp.int32, (1, count), 1)
+        position = ROW_BLOCK[g] * BLOCK + plane * PIECE + lax.rem(key, PIECE) + last * POS_STRIDE[order[2]]
+        for axis, stride in zip(order, SLOT_STRIDE, strict=True):
+            position = position + lax.rem(key // stride, 4) * POS_STRIDE[axis]
+        masks.append(position < limit)
+    keys = jnp.concatenate([buf[span, :] for span in spans], axis=0)
+    scores = dot_nt(qs[...], keys)
+    scores = jnp.where(jnp.concatenate(masks, axis=1), scores, neg_fill)
+    before = top[:, :1]
+    peak = jnp.maximum(before, jnp.max(scores, axis=1, keepdims=True))
+    factor = jnp.exp2((before - peak) * EXP2_SCALE)
+    expo = jnp.exp2((scores - peak) * EXP2_SCALE)
+    top[...] = jnp.broadcast_to(peak, (256, 128))
+    total[...] = total[...] * factor + jnp.sum(expo, axis=1, keepdims=True)
+    values = jnp.concatenate([buf[span, :RANK] for span in spans], axis=0)
+    acc[...] = acc[...] * factor + dot_nn(expo.astype(BF16), values)
 
 
 def kernel(
@@ -57,10 +91,12 @@
     q_dec,
     kv_new,
     lengths,
-    block_map,
     o_pre,
-    o_cache,
-    o_dec,
+    buf,
+    qs,
+    acc,
+    top,
+    total,
     tok_v,
     w_v,
     q_v,
@@ -71,16 +107,10 @@
     from_core,
     chip_sum,
     from_x,
-    buf,
     win,
-    qs,
     kn,
-    acc,
-    top,
-    total,
-    out_v,
-    cache_v,
-    dec_v,
+    pre_s,
+    pre_w,
     load_sem,
     core_send,
     core_recv,
@@ -90,7 +120,8 @@
     g_recv,
     f_send,
     f_recv,
-    out_sem,
+    l_send,
+    l_recv,
 ):
     ctx = lax.axis_index("ctx")
     grp = lax.axis_index("grp")
@@ -120,11 +151,12 @@
         "q": pltpu.make_async_copy(q_pre, q_v, load_sem.at[4]),
         "uv": pltpu.make_async_copy(w_uv, uv_v, load_sem.at[5]),
     }
-    for load in loads.values():
-        load.start()
+    loads["tok"].start()
+    loads["w"].start()
 
     barrier = pltpu.get_barrier_semaphore()
-    peers = [sibling] + [moved(axis, delta) for axis in "xyz" for delta in DELTAS]
+    across = [device(lax.rem(at["x"] + delta, 4), at["y"], at["z"], other) for delta in DELTAS]
+    peers = [sibling] + across + [moved(axis, delta) for axis in "xyz" for delta in DELTAS]
     for peer in peers:
         pl.semaphore_signal(barrier, inc=1, device_id=peer, device_id_type=MESH)
 
@@ -140,7 +172,7 @@
         freq = jnp.where(lane % 32 == i, value, freq)
     tables = []
     for g in range(GROUPS):
-        position = ctx * 512 + g * BLOCK + grp * PIECE + row
+        position = ctx * 512 + ROW_BLOCK[g] * BLOCK + grp * PIECE + row
         angle = position.astype(F32) * freq
         cosine = jnp.where(lane < ROPE, jnp.cos(angle), 0.0)
         sine = jnp.where(lane < ROPE, jnp.sin(angle), 0.0)
@@ -148,28 +180,32 @@
 
     loads["tok"].wait()
     loads["w"].wait()
+    for name in ("qd", "kv", "q", "uv"):
+        loads[name].start()
 
     core_copies = []
-    for g in range(GROUPS):
-        product = dot_nt(tok_v[g * BLOCK : (g + 1) * BLOCK, :], w_v[...])
+    x_copies = []
+
+    def project(g):
+        first = ROW_BLOCK[g] * BLOCK
+        product = dot_nt(tok_v[first : first + BLOCK, :], w_v[...])
         for x in range(4):
             for c in range(2):
                 at_row = (x * 2 + c) * PIECE
                 part[g, c, x * PIECE : (x + 1) * PIECE, :] = product[at_row : at_row + PIECE]
-        if g == 0:
-            pl.semaphore_wait(barrier, len(peers))
+
+    def to_core(g):
         copy = remote(part.at[g, other], from_core.at[g], core_send.at[g], core_recv.at[g], sibling)
         copy.start()
         core_copies.append(copy)
 
-    x_copies = []
-    for g in range(GROUPS):
+    def to_x(g):
         core_copies[g].wait_recv()
         chip_sum[g] = part[g, core] + from_core[g]
         for i, delta in enumerate(DELTAS):
-            to_x = lax.rem(at["x"] + delta, 4)
+            target = lax.rem(at["x"] + delta, 4)
             copy = remote(
-                chip_sum.at[g, pl.ds(pl.multiple_of(to_x * PIECE, PIECE), PIECE)],
+                chip_sum.at[g, pl.ds(pl.multiple_of(target * PIECE, PIECE), PIECE)],
                 from_x.at[g, i],
                 x_send.at[g * 3 + i],
                 x_recv.at[g * 3 + i],
@@ -177,6 +213,19 @@
             )
             copy.start()
             x_copies.append(copy)
+
+    project(0)
+    pl.semaphore_wait(barrier, len(peers))
+    to_core(0)
+    project(1)
+    to_core(1)
+    project(2)
+    to_core(2)
+    to_x(0)
+    project(3)
+    to_core(3)
+    for g in range(1, GROUPS):
+        to_x(g)
 
     sends = []
 
@@ -195,9 +244,6 @@
             new[first] = lax.rem(at[first] + delta * (1 - core), 4)
             new[second] = lax.rem(at[second] + delta * core, 4)
         return device(new["x"], new["y"], new["z"], core)
-
-    def base(g, plane):
-        return (plane * GROUPS + g) * GROUP_ROWS
 
     def rows_at(start, count):
         return buf.at[pl.ds(pl.multiple_of(start, PIECE), count)]
@@ -260,6 +306,32 @@
         for i, delta in enumerate(DELTAS):
             gather_send(g, i, own, PIECE, 0, delta)
 
+    def line_at(x, c):
+        return win.at[0, pl.ds(pl.multiple_of(4 * BLOCK + (x * 2 + c) * PIECE, PIECE), PIECE)]
+
+    line_to = [moved("x", delta) for delta in DELTAS] + across + [sibling]
+
+    def send_line():
+        own = base(0, core) + spots[0][2] * 256 + spots[0][1] * 64 + spots[0][0] * 16
+        for i, to in enumerate(line_to):
+            copy = remote(rows_at(own, PIECE), line_at(at["x"], core), l_send.at[i], l_recv.at[i], to)
+            copy.start()
+            sends.append(copy)
+        win[0, pl.ds(pl.multiple_of(4 * BLOCK + grp * PIECE, PIECE), PIECE), :] = buf[
+            pl.ds(pl.multiple_of(own, PIECE), PIECE), :
+        ]
+
+    def wait_line():
+        own = base(0, core) + spots[0][2] * 256 + spots[0][1] * 64 + spots[0][0] * 16
+        for i in range(len(line_to)):
+            x = at["x"] if i == 6 else lax.rem(at["x"] + 4 - DELTAS[i % 3], 4)
+            c = core if i < 3 else other
+            remote(rows_at(own, PIECE), line_at(x, c), l_send.at[i], l_recv.at[i], sibling).wait_recv()
+        for k in range(8):
+            target = 4 * BLOCK + k * PIECE
+            piece = win[0, target : target + PIECE, :]
+            win[1, target : target + PIECE, :] = pltpu.roll(piece.astype(F32), 64, 1).astype(BF16)
+
     def phase2(g):
         line = base(g, core) + spots[g][2] * 256 + spots[g][1] * 64
         for i, delta in enumerate(DELTAS):
@@ -321,43 +393,31 @@
 
     def prefill(b):
         first = ctx * 4 + b
-        qrow = lax.rem(lax.broadcasted_iota(jnp.int32, (4 * BLOCK, 2 * BLOCK), 0), BLOCK)
-        kcol = lax.broadcasted_iota(jnp.int32, (4 * BLOCK, 2 * BLOCK), 1)
+        qrow = lax.broadcasted_iota(jnp.int32, (BLOCK, 2 * BLOCK), 0)
+        kcol = lax.broadcasted_iota(jnp.int32, (BLOCK, 2 * BLOCK), 1)
         floor = jnp.where(first > 0, 0, BLOCK)
         allowed = (kcol >= floor) & (kcol - BLOCK <= qrow)
-        values = win[0, b * BLOCK : (b + 2) * BLOCK, :RANK]
-
-        def quad(j, carry):
-            for odd in range(2):
-                queries = jnp.concatenate(
-                    [
-                        q_v[
-                            b * BLOCK : (b + 1) * BLOCK,
-                            pl.ds(pl.multiple_of(j * (8 * WIDTH) + p * (2 * WIDTH) + odd * RANK, 128), WIDE),
-                        ]
-                        for p in range(4)
-                    ],
-                    axis=0,
-                )
-                scores = dot_nt(queries, win[odd, b * BLOCK : (b + 2) * BLOCK, :])
-                scores = jnp.where(allowed, scores, neg_fill)
+        mine = slice(b * BLOCK, (b + 1) * BLOCK)
+        for odd in range(2):
+            queries = jnp.concatenate(
+                [q_v[mine, p * 2 * WIDTH + odd * RANK : p * 2 * WIDTH + odd * RANK + WIDE] for p in range(8)], axis=0
+            )
+            pre_s[odd] = dot_nt(queries, win[odd, b * BLOCK : (b + 2) * BLOCK, :])
+        for odd in range(2):
+            for p in range(8):
+                rows = slice(p * BLOCK, (p + 1) * BLOCK)
+                scores = jnp.where(allowed, pre_s[odd, rows], neg_fill)
                 peak = jnp.max(scores, axis=1, keepdims=True)
                 expo = jnp.exp2((scores - peak) * EXP2_SCALE)
                 share = 1.0 / jnp.sum(expo, axis=1, keepdims=True)
-                weights = (expo * share).astype(BF16)
-                latent = dot_nn(weights, values).astype(BF16)
-                for p in range(4):
-                    column = pl.ds(pl.multiple_of(j * 1024 + (2 * p + odd) * 128, 128), 128)
-                    result = dot_nn(latent[p * BLOCK : (p + 1) * BLOCK], uv_v[:, column])
-                    out_v[b * BLOCK : (b + 1) * BLOCK, column] = result.astype(BF16)
-            return carry
-
-        lax.fori_loop(0, 2, quad, 0)
-        out = pltpu.make_async_copy(
-            out_v.at[pl.ds(b * BLOCK, BLOCK)], o_pre.at[pl.ds(b * BLOCK, BLOCK)], out_sem.at[b]
-        )
-        out.start()
-        return out
+                pre_w[odd, rows] = (expo * share).astype(BF16)
+        values = win[0, b * BLOCK : (b + 2) * BLOCK, :RANK]
+        for odd in range(2):
+            latent = dot_nn(pre_w[odd], values).astype(BF16)
+            for p in range(8):
+                column = slice((2 * p + odd) * 128, (2 * p + odd + 1) * 128)
+                result = dot_nn(latent[p * BLOCK : (p + 1) * BLOCK], uv_v[:, column])
+                o_pre[mine, column] = result.astype(BF16)
 
     def decode_start():
         loads["qd"].wait()
@@ -384,49 +444,12 @@
         total[...] = jnp.broadcast_to(jnp.sum(expo, axis=1, keepdims=True), (256, 128))
         acc[...] = dot_nn(expo.astype(BF16), kn[:, :RANK])
 
-    request = lax.rem(lax.broadcasted_iota(jnp.int32, (256, 1), 0), 16)
-    limit = jnp.zeros((256, 1), jnp.int32)
-    for r in range(16):
-        limit = jnp.where(request == r, lengths[r], limit)
-
-    def decode_chunk(plane, g):
-        start = base(g, plane)
-        key = lax.broadcasted_iota(jnp.int32, (1, GROUP_ROWS), 1)
-        position = g * BLOCK + plane * PIECE + lax.rem(key, PIECE)
-        for axis, stride in zip(ORDERS[g][plane], SLOT_STRIDE, strict=True):
-            position = position + lax.rem(key // stride, 4) * POS_STRIDE[axis]
-        scores = dot_nt(qs[...], buf[start : start + GROUP_ROWS, :])
-        scores = jnp.where(position < limit, scores, neg_fill)
-        before = top[:, :1]
-        peak = jnp.maximum(before, jnp.max(scores, axis=1, keepdims=True))
-        factor = jnp.exp2((before - peak) * EXP2_SCALE)
-        expo = jnp.exp2((scores - peak) * EXP2_SCALE)
-        top[...] = jnp.broadcast_to(peak, (256, 128))
-        total[...] = total[...] * factor + jnp.sum(expo, axis=1, keepdims=True)
-        acc[...] = acc[...] * factor + dot_nn(expo.astype(BF16), buf[start : start + GROUP_ROWS, :RANK])
-
-    def pick_pages(plane, g):
-        for owner in range(16):
-            target = owner * 32 + plane * PIECE
-            piece = cache_v[target : target + PIECE, :] if g else jnp.zeros((PIECE, WIDTH), BF16)
-            where = {"y": owner % 4, "z": owner // 4}
-            for x in range(4):
-                start = base(g, plane)
-                for axis, stride in zip(ORDERS[g][plane], SLOT_STRIDE, strict=True):
-                    start = start + (x if axis == "x" else where[axis]) * stride
-                mine = block_map[owner * 16 + g * 4 + x] == ctx
-                piece = jnp.where(mine, buf[start : start + PIECE, :WIDTH], piece)
-            cache_v[target : target + PIECE, :] = piece
-
-    def decode_end():
-        result = (acc[...] / total[:, :1]).astype(BF16)
-        for h in range(DEC_HEADS):
-            for s in range(2):
-                at_row = h * 32 + s * 16
-                dec_v[s, :, h * RANK : (h + 1) * RANK] = result[at_row : at_row + 16]
+    def decode(parts):
+        attend(parts, at, lengths, buf, qs, acc, top, total)
 
     finish_sum(0)
     phase1(0)
+    send_line()
     finish_sum(1)
     phase1(1)
     finish_sum(2)
@@ -442,44 +465,90 @@
     phase3(2)
     phase3(3)
     decode_start()
+    forward(0)
     loads["q"].wait()
     loads["uv"].wait()
+    wait_line()
     for g in range(GROUPS):
         passed(g, (0,))
-    copy_window(1, 2, at)
-    copy_window(2, 3, at)
-    copy_window(3, 4, at)
-    outs = []
-    outs.append(prefill(2))
-    for g in range(GROUPS):
-        forward(g)
-    outs.append(prefill(3))
-    for g in range(GROUPS):
-        near(g)
-    for g in range(GROUPS):
-        far(g)
-    for g in range(GROUPS):
-        passed(g, range(1, 7))
-    copy_window(0, 1, at)
+    for g in range(1, GROUPS):
+        copy_window(g, g, at)
+    prefill(1)
+    forward(1)
+    forward(2)
+    near(0)
+    prefill(2)
+    forward(3)
+    far(0)
+    prefill(3)
+    near(1)
+    near(2)
+    passed(0, range(1, 7))
     behind = lax.rem(ctx + 15, 16)
-    copy_window(3, 0, {"z": behind // 4, "y": lax.rem(behind, 4)})
-    outs.append(prefill(1))
-    outs.append(prefill(0))
-    for plane in range(2):
-        for g in range(GROUPS):
-            decode_chunk(plane, g)
-            pick_pages(plane, g)
-    out = pltpu.make_async_copy(cache_v, o_cache, out_sem.at[4])
-    out.start()
-    outs.append(out)
-    decode_end()
-    out = pltpu.make_async_copy(dec_v, o_dec, out_sem.at[5])
-    out.start()
-    outs.append(out)
+    copy_window(0, 0, {"z": behind // 4, "y": lax.rem(behind, 4)})
+    decode([(0, 0, None)])
+    decode([(1, 0, None)])
+    far(1)
+    far(2)
+    prefill(0)
+    near(3)
+    passed(1, range(1, 7))
+    decode([(0, 1, None)])
+    decode([(1, 1, None)])
+    passed(2, range(1, 7))
+    far(3)
+    decode([(0, 2, None)])
+    decode([(1, 2, None)])
+    passed(3, range(1, 5))
+    decode([(c, 3, offset) for c in range(2) for offset in (0, 1, 3)])
+    passed(3, range(5, 7))
     for copy in core_copies + x_copies + sends:
         copy.wait_send()
-    for out in outs:
-        out.wait()
+
+
+def finish(
+    pre, buf, qs, acc_in, top_in, total_in, lengths, block_map, o_pre, o_cache, o_dec, acc, top, total, cache, flipped, dec, sems
+):
+    ctx = lax.axis_index("ctx")
+    at = {"z": ctx // 4, "y": lax.rem(ctx, 4), "x": lax.axis_index("grp") // 2}
+    pre_copy = pltpu.make_async_copy(pre, o_pre, sems.at[0])
+    pre_copy.start()
+    acc[...] = acc_in[...]
+    top[...] = top_in[...]
+    total[...] = total_in[...]
+    attend([(0, 3, 2), (1, 3, 2)], at, lengths, buf, qs, acc, top, total)
+    result = (acc[...] / total[:, :1]).astype(BF16)
+    for h in range(DEC_HEADS):
+        for s in range(2):
+            at_row = h * 32 + s * 16
+            dec[s, :, h * RANK : (h + 1) * RANK] = result[at_row : at_row + 16]
+    dec_copy = pltpu.make_async_copy(dec, o_dec, sems.at[1])
+    dec_copy.start()
+
+    def take_page(owner, carry):
+        def look(j, found):
+            return jnp.where(block_map[owner * 16 + j] == ctx, j, found)
+
+        page = lax.fori_loop(0, 16, look, jnp.int32(0), unroll=True)
+        row_block = page // 4
+        where = {"x": lax.rem(page, 4), "y": lax.rem(owner, 4), "z": owner // 4}
+        for c in range(2):
+            start = jnp.int32(0)
+            for k in range(GROUPS):
+                here = base(k, c)
+                for axis, stride in zip(ORDERS[k][c], SLOT_STRIDE, strict=True):
+                    here = here + where[axis] * stride
+                start = jnp.where(row_block == ROW_BLOCK[k], here, start)
+            target = pl.multiple_of(owner * 32 + c * PIECE, PIECE)
+            cache[pl.ds(target, PIECE), :] = buf[pl.ds(pl.multiple_of(start, PIECE), PIECE), :]
+        return carry
+
+    lax.fori_loop(0, 16, take_page, 0)
+    flipped[...] = cache[...].T[:WIDTH]
+    cache_copy = pltpu.make_async_copy(flipped, o_cache, sems.at[2])
+    cache_copy.start()
+    for copy in (pre_copy, dec_copy, cache_copy):
+        copy.wait()
 
 
 def shards(tokens, w_dkv, latent_gain, q_pre, w_uv, q_dec, kv_new, lengths, block_map):
@@ -487,15 +556,18 @@
     vmem = pl.BlockSpec(memory_space=pltpu.VMEM)
     smem = pl.BlockSpec(memory_space=pltpu.SMEM)
     sems = pltpu.SemaphoreType.DMA
-    return pl.pallas_call(
+    results = pl.pallas_call(
         kernel,
         out_shape=(
-            jax.ShapeDtypeStruct((512, 2048), BF16),
-            jax.ShapeDtypeStruct((512, WIDTH), BF16),
-            jax.ShapeDtypeStruct((2, 16, 4096), BF16),
+            pltpu.VMEM((512, 2048), BF16),
+            pltpu.VMEM((2 * GROUPS * GROUP_ROWS, WIDE), BF16),
+            pltpu.VMEM((256, WIDE), BF16),
+            pltpu.VMEM((256, RANK), F32),
+            pltpu.VMEM((256, 128), F32),
+            pltpu.VMEM((256, 128), F32),
         ),
-        in_specs=[anywhere, anywhere, vmem, anywhere, anywhere, anywhere, anywhere, smem, smem],
-        out_specs=(anywhere, anywhere, anywhere),
+        in_specs=[anywhere, anywhere, vmem, anywhere, anywhere, anywhere, anywhere, smem],
+        out_specs=(vmem,) * 6,
         scratch_shapes=[
             pltpu.VMEM((512, 896), BF16),
             pltpu.VMEM((WIDTH, 896), BF16),
@@ -507,16 +579,10 @@
             pltpu.VMEM((GROUPS, 64, WIDTH), F32),
             pltpu.VMEM((GROUPS, 64, WIDTH), F32),
             pltpu.VMEM((GROUPS, 3, PIECE, WIDTH), F32),
-            pltpu.VMEM((2 * GROUPS * GROUP_ROWS, WIDE), BF16),
             pltpu.VMEM((2, 5 * BLOCK, WIDE), BF16),
-            pltpu.VMEM((256, WIDE), BF16),
             pltpu.VMEM((32, WIDE), BF16),
-            pltpu.VMEM((256, RANK), F32),
-            pltpu.VMEM((256, 128), F32),
-            pltpu.VMEM((256, 128), F32),
-            pltpu.VMEM((512, 2048), BF16),
-            pltpu.VMEM((512, WIDTH), BF16),
-            pltpu.VMEM((2, 16, 4096), BF16),
+            pltpu.VMEM((2, 1024, 256), F32),
+            pltpu.VMEM((2, 1024, 256), BF16),
             sems((6,)),
             sems((GROUPS,)),
             sems((GROUPS,)),
@@ -526,12 +592,34 @@
             sems((GROUPS * 12,)),
             sems((GROUPS * 7,)),
             sems((GROUPS * 7,)),
-            sems((6,)),
+            sems((7,)),
+            sems((7,)),
         ],
         compiler_params=pltpu.CompilerParams(
-            collective_id=0, has_side_effects=True, vmem_limit_bytes=56 * 1024 * 1024
+            collective_id=0, has_side_effects=True, vmem_limit_bytes=48 * 1024 * 1024
         ),
-    )(tokens, w_dkv.T, latent_gain.reshape(1, RANK), q_pre, w_uv, q_dec, kv_new, lengths, block_map)
+    )(tokens, w_dkv.T, latent_gain.reshape(1, RANK), q_pre, w_uv, q_dec, kv_new, lengths)
+    pre, cache, dec = pl.pallas_call(
+        finish,
+        out_shape=(
+            jax.ShapeDtypeStruct((512, 2048), BF16),
+            jax.ShapeDtypeStruct((WIDTH, 512), BF16),
+            jax.ShapeDtypeStruct((2, 16, 4096), BF16),
+        ),
+        in_specs=[vmem] * 6 + [smem, smem],
+        out_specs=(anywhere, anywhere, anywhere),
+        scratch_shapes=[
+            pltpu.VMEM((256, RANK), F32),
+            pltpu.VMEM((256, 128), F32),
+            pltpu.VMEM((256, 128), F32),
+            pltpu.VMEM((512, WIDE), BF16),
+            pltpu.VMEM((WIDTH, 512), BF16),
+            pltpu.VMEM((2, 16, 4096), BF16),
+            sems((3,)),
+        ],
+        compiler_params=pltpu.CompilerParams(vmem_limit_bytes=24 * 1024 * 1024),
+    )(*results, lengths, block_map)
+    return pre, cache.T, dec
 
 
 def solution(mesh):

time: 77.2 us -> 59.1 us (0.77)
  Pallas kernels: 70.3 us -> 58.1 us
  local copies, waits for them, and re-layouts: 6.04 us -> 0.01 us
    pallas_call x1 -> x2, Pallas kernels: 70.3 us -> 58.1 us  [the longest x1 54.9 us: shards(): pl.pallas_call(kernel, out_shape=(pltpu.VMEM((512, 2048), BF16), pltpu.VM...]
    unnamed x4, local copies, waits for them, and re-layouts: 3.91 us -> 0.01 us
    pallas_call x1 -> x0, local copies, waits for them, and re-layouts: 2.13 us -> none  [shards(): pl.pallas_call(kernel, out_shape=(jax.ShapeDtypeStruct((512, 2048), BF16)...]
where the time goes in v2:
time: 59.1 us; the launch traced here: 58.9 us
  Pallas kernels  58.1 us (98%)
  between operations  0.83 us (1%)
    pallas_call x1, Pallas kernels, shards(): pl.pallas_call(kernel, out_shape=(pltpu.VMEM((512, 2048), BF16), pltpu.VM...  54.9 us
    pallas_call x1, Pallas kernels, shards(): pl.pallas_call(finish, out_shape=(jax.ShapeDtypeStruct((512, 2048), BF16)...  3.2 us

profile of v2, /device:TPU:1, one launch (start us, length us, event | category | flops | bytes accessed | tf_op | source)
XLA Modules:
  0.0 58.9 jit_solution(9016019063573131085)
XLA Ops:
  0.6 0.0 copy-start
  0.6 0.0 copy-start.1
  0.7 54.9 %shard_map.112 = (bf16[512,2048]{1,0:T(8,128)(2,1)S(1)}, bf16[8192,640]{1,0:T(8,128)(2,1)S(1)}, bf16[256,640]{1,0:T(8,128)(2,1)S(1)}, f32[256,512]{1,0:T(8,128)S...) custom-call(bf16[512,896]{1,0:T(8,128)(2,1)} %tokens.1, bf16[576,896]{1,0:T(8,128)(2,1)} %bitcast.3, ...), custom_call_target="tpu_custom_call" | custom-call | tf_op jit(solution)/shard_map/pallas_call | solution.py:559
  55.5 0.0 copy-done
  55.5 0.0 copy-done.1
  55.6 3.2 %shard_map.113 = (bf16[512,2048]{1,0:T(8,128)(2,1)}, bf16[576,512]{1,0:T(8,128)(2,1)}, bf16[2,16,4096]{2,1,0:T(8,128)(2,1)}) custom-call(bf16[512,2048]{1,0:T(8,128)(2,1)S(1)} %get-tuple-element.12.pre, bf16[8192,640]{1,0:T(8,128)(2,1)S(1)} %get-tuple-element.13.buf, bf16[256,640]{1,0:T(8,128)(2,1)S(1)} %get-tuple-element.14.qs, ...), custom_call_target="tpu_custom_call" | custom-call | tf_op jit(solution)/shard_map/pallas_call | solution.py:602
Async XLA Ops:
  0.6 54.9 %copy-start = (s32[16]{0:T(128)S(1)}, s32[16]{0:T(128)}, u32[]{:S(2)}) copy-start(s32[16]{0:T(128)} %lengths.3) | copy-start | bytes 196
  0.6 54.9 %copy-start.1 = (s32[256]{0:T(256)S(1)}, s32[256]{0:T(256)}, u32[]{:S(2)}) copy-start(s32[256]{0:T(256)} %block_map.1) | copy-start | bytes 3076

commit v3 on v2

--- a/solution.py
+++ b/solution.py
@@ -469,8 +469,9 @@
     loads["q"].wait()
     loads["uv"].wait()
     wait_line()
-    for g in range(GROUPS):
+    for g in range(GROUPS - 1):
         passed(g, (0,))
+    passed(3, (0,))
     for g in range(1, GROUPS):
         copy_window(g, g, at)
     prefill(1)
@@ -478,8 +479,8 @@
     forward(2)
     near(0)
     prefill(2)
+    far(0)
     forward(3)
-    far(0)
     prefill(3)
     near(1)
     near(2)
@@ -488,20 +489,19 @@
     copy_window(0, 0, {"z": behind // 4, "y": lax.rem(behind, 4)})
     decode([(0, 0, None)])
     decode([(1, 0, None)])
+    near(3)
+    prefill(0)
+    passed(1, range(1, 5))
+    decode([(c, 1, offset) for c in range(2) for offset in (0, 1, 3)])
     far(1)
     far(2)
-    prefill(0)
-    near(3)
-    passed(1, range(1, 7))
-    decode([(0, 1, None)])
-    decode([(1, 1, None)])
-    passed(2, range(1, 7))
+    passed(2, range(1, 5))
+    decode([(c, 2, offset) for c in range(2) for offset in (0, 1, 3)])
     far(3)
-    decode([(0, 2, None)])
-    decode([(1, 2, None)])
     passed(3, range(1, 5))
     decode([(c, 3, offset) for c in range(2) for offset in (0, 1, 3)])
-    passed(3, range(5, 7))
+    for g in range(1, GROUPS):
+        passed(g, range(5, 7))
     for copy in core_copies + x_copies + sends:
         copy.wait_send()
 
@@ -516,7 +516,7 @@
     acc[...] = acc_in[...]
     top[...] = top_in[...]
     total[...] = total_in[...]
-    attend([(0, 3, 2), (1, 3, 2)], at, lengths, buf, qs, acc, top, total)
+    attend([(c, g, 2) for c in range(2) for g in (1, 2, 3)], at, lengths, buf, qs, acc, top, total)
     result = (acc[...] / total[:, :1]).astype(BF16)
     for h in range(DEC_HEADS):
         for s in range(2):

time: 59.1 us -> 58.6 us (level)
    pallas_call x1, Pallas kernels: 54.9 us -> 53.6 us  [shards(): pl.pallas_call(kernel, out_shape=(pltpu.VMEM((512, 2048), BF16), pltpu.VM...]
    pallas_call x1, Pallas kernels: 3.2 us -> 3.98 us  [shards(): pl.pallas_call(finish, out_shape=(jax.ShapeDtypeStruct((512, 2048), BF16)...]
where the time goes in v3:
time: 58.6 us; the launch traced here: 58.4 us
  Pallas kernels  57.6 us (98%)
  between operations  0.83 us (1%)
    pallas_call x1, Pallas kernels, shards(): pl.pallas_call(kernel, out_shape=(pltpu.VMEM((512, 2048), BF16), pltpu.VM...  53.6 us
    pallas_call x1, Pallas kernels, shards(): pl.pallas_call(finish, out_shape=(jax.ShapeDtypeStruct((512, 2048), BF16)...  3.98 us

profile of v3, /device:TPU:1, one launch (start us, length us, event | category | flops | bytes accessed | tf_op | source)
XLA Modules:
  0.0 58.4 jit_solution(18328594063029095072)
XLA Ops:
  0.6 0.0 copy-start
  0.6 0.0 copy-start.1
  0.7 53.6 %shard_map.112 = (bf16[512,2048]{1,0:T(8,128)(2,1)S(1)}, bf16[8192,640]{1,0:T(8,128)(2,1)S(1)}, bf16[256,640]{1,0:T(8,128)(2,1)S(1)}, f32[256,512]{1,0:T(8,128)S...) custom-call(bf16[512,896]{1,0:T(8,128)(2,1)} %tokens.1, bf16[576,896]{1,0:T(8,128)(2,1)} %bitcast.3, ...), custom_call_target="tpu_custom_call" | custom-call | tf_op jit(solution)/shard_map/pallas_call | solution.py:559
  54.3 0.0 copy-done
  54.3 0.0 copy-done.1
  54.3 4.0 %shard_map.113 = (bf16[512,2048]{1,0:T(8,128)(2,1)}, bf16[576,512]{1,0:T(8,128)(2,1)}, bf16[2,16,4096]{2,1,0:T(8,128)(2,1)}) custom-call(bf16[512,2048]{1,0:T(8,128)(2,1)S(1)} %get-tuple-element.12.pre, bf16[8192,640]{1,0:T(8,128)(2,1)S(1)} %get-tuple-element.13.buf, bf16[256,640]{1,0:T(8,128)(2,1)S(1)} %get-tuple-element.14.qs, ...), custom_call_target="tpu_custom_call" | custom-call | tf_op jit(solution)/shard_map/pallas_call | solution.py:602
Async XLA Ops:
  0.6 53.6 %copy-start = (s32[16]{0:T(128)S(1)}, s32[16]{0:T(128)}, u32[]{:S(2)}) copy-start(s32[16]{0:T(128)} %lengths.3) | copy-start | bytes 196
  0.6 53.6 %copy-start.1 = (s32[256]{0:T(256)S(1)}, s32[256]{0:T(256)}, u32[]{:S(2)}) copy-start(s32[256]{0:T(256)} %block_map.1) | copy-start | bytes 3076

commit v4 on v3

--- a/solution.py
+++ b/solution.py
@@ -489,17 +489,17 @@
     copy_window(0, 0, {"z": behind // 4, "y": lax.rem(behind, 4)})
     decode([(0, 0, None)])
     decode([(1, 0, None)])
-    near(3)
     prefill(0)
     passed(1, range(1, 5))
     decode([(c, 1, offset) for c in range(2) for offset in (0, 1, 3)])
+    near(3)
     far(1)
-    far(2)
     passed(2, range(1, 5))
     decode([(c, 2, offset) for c in range(2) for offset in (0, 1, 3)])
-    far(3)
+    far(2)
     passed(3, range(1, 5))
     decode([(c, 3, offset) for c in range(2) for offset in (0, 1, 3)])
+    far(3)
     for g in range(1, GROUPS):
         passed(g, range(5, 7))
     for copy in core_copies + x_copies + sends:

time: 58.6 us -> 60.1 us (1.026)
  Pallas kernels: 57.6 us -> 59.1 us
    pallas_call x1, Pallas kernels: 53.6 us -> 55.1 us  [shards(): pl.pallas_call(kernel, out_shape=(pltpu.VMEM((512, 2048), BF16), pltpu.VM...]
where the time goes in v4:
time: 60.1 us; the launch traced here: 59.9 us
  Pallas kernels  59.1 us (98%)
  between operations  0.83 us (1%)
    pallas_call x1, Pallas kernels, shards(): pl.pallas_call(kernel, out_shape=(pltpu.VMEM((512, 2048), BF16), pltpu.VM...  55.1 us
    pallas_call x1, Pallas kernels, shards(): pl.pallas_call(finish, out_shape=(jax.ShapeDtypeStruct((512, 2048), BF16)...  3.98 us

profile of v4, /device:TPU:1, one launch (start us, length us, event | category | flops | bytes accessed | tf_op | source)
XLA Modules:
  0.0 59.9 jit_solution(13647146224699181705)
XLA Ops:
  0.6 0.0 copy-start
  0.6 0.0 copy-start.1
  0.7 55.1 %shard_map.112 = (bf16[512,2048]{1,0:T(8,128)(2,1)S(1)}, bf16[8192,640]{1,0:T(8,128)(2,1)S(1)}, bf16[256,640]{1,0:T(8,128)(2,1)S(1)}, f32[256,512]{1,0:T(8,128)S...) custom-call(bf16[512,896]{1,0:T(8,128)(2,1)} %tokens.1, bf16[576,896]{1,0:T(8,128)(2,1)} %bitcast.3, ...), custom_call_target="tpu_custom_call" | custom-call | tf_op jit(solution)/shard_map/pallas_call | solution.py:559
  55.8 0.0 copy-done
  55.8 0.0 copy-done.1
  55.8 4.0 %shard_map.113 = (bf16[512,2048]{1,0:T(8,128)(2,1)}, bf16[576,512]{1,0:T(8,128)(2,1)}, bf16[2,16,4096]{2,1,0:T(8,128)(2,1)}) custom-call(bf16[512,2048]{1,0:T(8,128)(2,1)S(1)} %get-tuple-element.12.pre, bf16[8192,640]{1,0:T(8,128)(2,1)S(1)} %get-tuple-element.13.buf, bf16[256,640]{1,0:T(8,128)(2,1)S(1)} %get-tuple-element.14.qs, ...), custom_call_target="tpu_custom_call" | custom-call | tf_op jit(solution)/shard_map/pallas_call | solution.py:602
Async XLA Ops:
  0.6 55.1 %copy-start = (s32[16]{0:T(128)S(1)}, s32[16]{0:T(128)}, u32[]{:S(2)}) copy-start(s32[16]{0:T(128)} %lengths.3) | copy-start | bytes 196
  0.6 55.1 %copy-start.1 = (s32[256]{0:T(256)S(1)}, s32[256]{0:T(256)}, u32[]{:S(2)}) copy-start(s32[256]{0:T(256)} %block_map.1) | copy-start | bytes 3076
